TPU v7x, 32 devices: a whole 2x2x4 slice. The times are simulated.
32 devices in a mesh: seq: 16 (over z, y, core), width: 2 (over x).
Axes of the slice: x: 2, y: 2, z: 4, core: 2. Of those that a mesh axis runs over, the one named last changes fastest.
Arguments:
- tokens: bfloat16 [16384, 16384], P('seq', 'width'), may hold values from -6 to 6
- panel_weights: bfloat16 [2, 16384, 1024], P(None, 'width', 'seq'), may hold values from -0.046875 to 0.046875
- panel_scales: float32 [2, 1024, 1024], P(None, 'width', 'seq'), may hold values from 0.4 to 2.5
- doc_lengths: int32 [16, 8], P('seq'), may hold values from 0 to 1024, as said below
Outputs:
- hidden: float32 [16384, 1024], P(('seq', 'width'))
Inputs may be any that keep to these rules, and one draw needn't show every extreme that they name: `doc_lengths`: each row sums to at most 1024; some row holds one document of exactly 1024; documents may be empty.
All inputs are finite; a program needn't handle non-finite values.
Results may differ from a plain program's by a relative error of at most 0.014.
Values may be sent and summed in bfloat16 or wider, within the bound.
A program may use at most 128 MiB of HBM per device.

v0:
```python
import jax
import jax.numpy as jnp
from jax import lax
from jax.sharding import PartitionSpec as P


def gathered_then(x, axis, dim, block):
    whole = lax.all_gather(x, axis, axis=dim, tiled=True)
    return block(whole, jnp.int32(0))


def per_device(tokens, panel_weights, panel_scales, doc_lengths):
    rows_here = tokens.shape[0]
    width_count = lax.axis_size("width")
    share = rows_here // width_count
    live_count = jnp.sum(doc_lengths)

    def product(pieces):
        weights, scales = pieces
        spread = jnp.repeat(scales, 16, axis=1)
        weights_deq = (weights.astype(jnp.float32) * spread).astype(jnp.bfloat16)
        partial_value = jnp.einsum(
            "td,gdc->tgc", tokens, weights_deq, preferred_element_type=jnp.float32
        )
        return partial_value

    summed = gathered_then(
        (panel_weights, panel_scales.astype(jnp.bfloat16)),
        "seq",
        2,
        lambda piece, start: product((piece[0], piece[1].astype(jnp.float32))),
    )
    summed = lax.psum_scatter(summed, "width", scatter_dimension=0, tiled=True)
    mixed = jax.nn.silu(summed[:, 0, :]) * summed[:, 1, :]
    position = lax.axis_index("width") * share + jnp.arange(share, dtype=jnp.int32)
    keep = position < live_count
    return jnp.where(keep[:, None], mixed, jnp.zeros_like(mixed))


def solution(mesh):
    in_specs = (P("seq", "width"), P(None, "width", "seq"), P(None, "width", "seq"), P("seq", None))
    out_specs = P(("seq", "width"), None)
    return jax.shard_map(
        per_device, mesh=mesh, in_specs=in_specs, out_specs=out_specs, check_vma=False
    )
```

profile of v0, /device:TPU:0, one launch (start us, length us, event | category | flops | bytes accessed | tf_op | source)
XLA Modules:
  0.0 481.2 jit_solution(3017127130118802450)
XLA Ops:
  6.5 0.0 all-gather.5.cloned.1.call-start
  6.5 1.6 convert_element_type.13
  8.2 0.0 all-gather.5.cloned.1.call-update
  8.2 0.0 all-gather.3.cloned.1.call-start
  8.2 5.1 %copy.10 = bf16[2,8192,64]{1,0,2:T(2,128)(2,1)} copy(bf16[2,8192,64]{1,2,0:T(8,128)(2,1)} %param.5) | data formatting | bytes 4194304 | tf_op args[1]
  13.3 0.0 all-gather.3.cloned.1.call-update
  13.4 0.2 reduce-scatter.2.cloned.1.call-start
  13.6 40.1 %all-gather.5.cloned.1.call-done = bf16[2,512,1024]{1,2,0:T(8,128)(2,1)} async-done(((bf16[2,512,64]{1,2,0:T(8,128)(2,1)}), bf16[2,512,1024]{1,2,0:T(8,128)(2,1)}) %all-gather.5.cloned.1.call-update) | async-done | bytes 2097168 | tf_op jit(solution)/shard_map/all_gather | solution.py:8
  53.7 4.2 copy.12
  57.9 164.3 %all-gather.3.cloned.1.call-done = bf16[2,8192,1024]{1,0,2:T(2,128)(2,1)} async-done(((bf16[2,8192,64]{1,0,2:T(2,128)(2,1)}), bf16[2,8192,1024]{1,0,2:T(2,128)(2,1)}) %all-gather.3.cloned.1.call-update) | async-done | bytes 33554448 | tf_op jit(solution)/shard_map/all_gather | solution.py:8
  222.2 80.4 %copy.11 = bf16[2,8192,1024]{2,1,0:T(8,128)(2,1)} copy(bf16[2,8192,1024]{1,0,2:T(2,128)(2,1)} %all-gather.3.cloned.1.call-done) | data formatting | bytes 67108864 | tf_op jit(solution)/shard_map/all_gather | solution.py:8
  302.5 24.4 %fusion = bf16[2,8192,1024]{2,1,0:T(8,128)(2,1)} fusion(bf16[2,8192,1024]{2,1,0:T(8,128)(2,1)} %copy.11, f32[2,512,1024]{2,1,0:T(8,128)} %copy.12), kind=kLoop, calls=%fused_computation.1 | loop fusion | flops 50331648 | bytes 71303168 | tf_op jit(solution)/shard_map/convert_element_type | solution.py:21
  326.9 43.7 %fusion.3 = f32[1024,2,1024]{0,2,1:T(8,128)} fusion(bf16[2,8192,1024]{2,1,0:T(8,128)(2,1)} %fusion, bf16[1024,8192]{1,0:T(8,128)(2,1)} %param.4), kind=kOutput, calls=%fused_computation.4 | convolution fusion | flops 34359738368 | bytes 58720256 | tf_op jit(solution)/shard_map/td,gdc->tgc/dot_general | solution.py:22
  370.7 0.0 copy-start
  370.7 0.0 reduce-scatter.2.cloned.1.call-update
  370.7 0.6 copy-done
  371.3 0.6 reduce_sum.9
  372.0 0.7 add_compare_fusion
  372.6 97.5 %reduce-scatter.2.cloned.1.call-done = f32[512,2,1024]{0,2,1:T(8,128)} async-done(((f32[1024,2,1024]{0,2,1:T(8,128)}), f32[512,2,1024]{0,2,1:T(8,128)}) %reduce-scatter.2.cloned.1.call-update) | async-done | bytes 4194320 | tf_op jit(solution)/shard_map/reduce_scatter | solution.py:33
  470.1 2.8 fusion.7
  472.9 1.8 copy.14
Async XLA Ops:
  6.5 47.2 %all-gather.5.cloned.1.call-start = ((), (), s32[]{:S(2)}) async-start(), calls=%async_computation.2 | async-start | bytes 2228224 | tf_op jit(solution)/shard_map/all_gather | solution.py:8
  8.2 214.0 %all-gather.3.cloned.1.call-start = ((), (), s32[]{:S(2)}) async-start(), calls=%async_computation.1 | async-start | bytes 35651584 | tf_op jit(solution)/shard_map/all_gather | solution.py:8
  13.4 456.8 %reduce-scatter.2.cloned.1.call-start = ((), (), s32[]{:S(2)}) async-start(), calls=%async_computation.3 | async-start | bytes 12582912 | tf_op jit(solution)/shard_map/reduce_scatter | solution.py:33
  370.7 0.7 copy-start
Sparse Core Ops, SparseCore 0:
  9.5 44.1 all-gather.4
  55.3 166.8 all-gather.2
  370.8 99.2 reduce-scatter.1
where the time goes:
time: 484 us; the launch traced here: 481 us
  waiting for transfers between devices  302 us (62%)
  local copies, waits for them, and re-layouts  92.1 us (19%)
  matrix products  43.7 us (9%)
  other arithmetic  30.1 us (6%)
  between operations  13.1 us (3%)
    all_gather x2, waiting for transfers between devices, gathered_then(): whole = lax.all_gather(x, axis, axis=dim, tiled=True)  204 us
    reduce_scatter x1, waiting for transfers between devices, per_device(): summed = lax.psum_scatter(summed, 'width', scatter_dimension=0, tiled=True)  97.5 us
    all_gather x1, local copies, waits for them, and re-layouts, gathered_then(): whole = lax.all_gather(x, axis, axis=dim, tiled=True)  80.4 us
    dot_general x1, matrix products, product(): jnp.einsum('td,gdc->tgc', tokens, weights_deq, preferred_element_type=jnp...  43.7 us
    convert_element_type x1, other arithmetic, product(): weights_deq = (weights.astype(jnp.float32) * spread).astype(jnp.bfloat16)  24.4 us
  transfers between devices with their start and end apart: 3, of which 3 were waited for; matrix products, arithmetic and copies ran while one was open for 2% of the time, Pallas kernels for 0%

commit v1 on v0

v1 whole, which is shorter than its diff:
```python
import functools

import jax
import jax.numpy as jnp
from jax import lax
from jax.experimental import pallas as pl
from jax.experimental.pallas import tpu as pltpu
from jax.sharding import PartitionSpec as P

MESH = pl.DeviceIdType.MESH
GROUP = 16
LEFT, RIGHT, ACROSS, SIBLING = range(4)


def pick(values, at):
    found = jnp.int32(values[0])
    for k in range(1, len(values)):
        found = jnp.where(at == k, jnp.int32(values[k]), found)
    return found


def kernel(
    n_seq, n_width, pieces,
    weights, scales, tokens, out,
    gathered, tok, spread_mat, acc, keep_up, send_buf, recv_buf,
    send_sem, recv_sem, x_send, x_recv, w_sem, tok_sem,
):
    n_z = n_seq // 4
    me, wid = lax.axis_index("seq"), lax.axis_index("width")
    core, chip = lax.rem(me, 2), me // 2
    y, z = lax.rem(chip, 2), chip // 2
    far = 1 - y
    rows, depth = weights.shape[1], weights.shape[2]
    per_half = pieces // 2
    r_piece = rows // per_half
    n_tok = tokens.shape[0]
    share = n_tok // n_width
    n_cols = 4 * rows

    def seq_of(zz, yy, cc):
        return {"seq": (zz * 2 + yy) * 2 + cc}

    target = {
        LEFT: seq_of(lax.rem(z + n_z - 1, n_z), y, core),
        RIGHT: seq_of(lax.rem(z + 1, n_z), y, core),
        ACROSS: seq_of(z, far, core),
        SIBLING: seq_of(z, y, 1 - core),
    }

    def block(c, p, half):
        return gathered.at[c, p // per_half, half, pl.ds((p % per_half) * r_piece, r_piece), :]

    def copy(c, p, way):
        return pltpu.make_async_remote_copy(
            src_ref=block(c, p, core), dst_ref=block(c, p, core),
            send_sem=send_sem.at[way, c, p], recv_sem=recv_sem.at[core, c, p],
            device_id=target[way], device_id_type=MESH,
        )

    def arrived(c, p, half):
        pltpu.make_async_remote_copy(
            src_ref=block(c, p, half), dst_ref=block(c, p, half),
            send_sem=send_sem.at[SIBLING, c, p], recv_sem=recv_sem.at[half, c, p],
            device_id=target[SIBLING], device_id_type=MESH,
        ).wait_recv()

    def x_copy(d, c):
        return pltpu.make_async_remote_copy(
            src_ref=send_buf.at[d - 1, c], dst_ref=recv_buf.at[d - 1, c],
            send_sem=x_send.at[d - 1, c], recv_sem=x_recv.at[d - 1, c],
            device_id={"width": lax.rem(wid + d, n_width)}, device_id_type=MESH,
        )

    w_copies = [
        pltpu.make_async_copy(weights.at[g], gathered.at[chip, g, core], w_sem.at[g])
        for g in range(2)
    ]
    for c in w_copies:
        c.start()
    tok_copy = pltpu.make_async_copy(tokens, tok, tok_sem)
    tok_copy.start()

    barrier = pltpu.get_barrier_semaphore()
    for way in range(4):
        pl.semaphore_signal(barrier, inc=1, device_id=target[way], device_id_type=MESH)
    for d in range(1, n_width):
        pl.semaphore_signal(
            barrier, inc=1, device_id={"width": lax.rem(wid + d, n_width)}, device_id_type=MESH
        )

    chunk = spread_mat.shape[0]
    wide = chunk * GROUP
    at_row = lax.broadcasted_iota(jnp.int32, (chunk, wide), 0)
    at_col = lax.broadcasted_iota(jnp.int32, (chunk, wide), 1)
    first_col = at_row * GROUP
    spread_mat[...] = jnp.where(
        (at_col >= first_col) & (at_col < first_col + GROUP), 1.0, 0.0
    ).astype(jnp.bfloat16)

    pl.semaphore_wait(barrier, 4 + n_width - 1)

    for p in range(pieces):
        g, row = p // per_half, (p % per_half) * r_piece
        if p % per_half == 0:
            w_copies[g].wait()

        @pl.loop(0, scales.shape[2] // chunk)
        def _(j):
            s = scales[g, pl.ds(row, r_piece), pl.ds(pl.multiple_of(j * chunk, chunk), chunk)]
            high = s.astype(jnp.bfloat16)
            rest = s - high.astype(jnp.float32)
            mid = rest.astype(jnp.bfloat16)
            low = (rest - mid.astype(jnp.float32)).astype(jnp.bfloat16)
            parts = jnp.dot(
                jnp.concatenate([high, mid, low], axis=0), spread_mat[...],
                preferred_element_type=jnp.float32,
            )
            spread = parts[:r_piece] + parts[r_piece:2 * r_piece] + parts[2 * r_piece:]
            cols = pl.ds(pl.multiple_of(j * wide, wide), wide)
            w = gathered[chip, g, core, pl.ds(row, r_piece), cols].astype(jnp.float32)
            gathered[chip, g, core, pl.ds(row, r_piece), cols] = (w * spread).astype(jnp.bfloat16)

        @pl.when(z > 0)
        def _():
            copy(chip, p, LEFT).start()

        @pl.when(z < n_z - 1)
        def _():
            copy(chip, p, RIGHT).start()

        copy(chip, p, ACROSS).start()
        copy(chip, p, SIBLING).start()

    tok_copy.wait()

    k_step = min(1024, depth)

    def compute(c):
        for p in range(pieces):
            arrived(c, p, 1 - core)

        def dot(k):
            at = pl.ds(pl.multiple_of(k * k_step, k_step), k_step)
            b = gathered[c, :, :, :, at].reshape(n_cols, k_step)
            return lax.dot_general(
                tok[:, at], b, (((1,), (1,)), ((), ())), preferred_element_type=jnp.float32
            )

        acc[...] = dot(0)

        @pl.loop(1, depth // k_step)
        def _(k):
            acc[...] += dot(k)

        mine = pl.ds(pl.multiple_of(wid * share, share), share)
        half_cols = n_cols // 2
        out[c] = acc[mine, :half_cols]
        keep_up[c] = acc[mine, half_cols:]
        for d in range(1, n_width):
            other = pl.ds(pl.multiple_of(lax.rem(wid + d, n_width) * share, share), share)
            send_buf[d - 1, c] = acc[other, :].astype(jnp.bfloat16)
            x_copy(d, c).start()

    def finish(c):
        half_cols = n_cols // 2
        for d in range(1, n_width):
            x_copy(d, c).wait_recv()
        gate, up = out[c], keep_up[c]
        for d in range(1, n_width):
            both = recv_buf[d - 1, c].astype(jnp.float32)
            gate, up = gate + both[:, :half_cols], up + both[:, half_cols:]
        out[c] = gate / (1.0 + jnp.exp(-gate)) * up

    orders = []
    for zz in range(n_z):
        order = [zz]
        for r in range(1, n_z):
            order += [b for b in (zz - r, zz + r) if 0 <= b < n_z]
        orders.append(order)
    nearest = [pick([orders[zz][k] for zz in range(n_z)], z) for k in range(n_z)]
    half_way = n_z // 2
    lent = jnp.where(z < half_way, z + 1, z - 1)
    lend_left = (z > 0) & (z - 1 < half_way)
    lend_right = (z < n_z - 1) & (z + 1 >= half_way)
    lent_pieces = range(pieces // 2, pieces)

    def over_y(k, p):
        return nearest[k] != lent if p in lent_pieces and k > 0 else z >= 0

    def blocks_of(r):
        found = []
        if 0 < r < n_z:
            found.append((z - r >= 0, (z - r) * 2 + y))
            found.append((z + r < n_z, (z + r) * 2 + y))
        if r > 0:
            whole = nearest[r - 1] != lent if r > 1 else z >= 0
            found.append((whole, nearest[r - 1] * 2 + far))
        else:
            found.append((z >= 0, chip))
        return found

    def guarded(f, cond, c):
        @pl.when(cond)
        def _():
            f(c)

    for r in range(1, n_z + 1):
        for p in range(pieces):
            if r < n_z:
                from_left, from_right = (z - r) * 2 + y, (z + r) * 2 + y

                @pl.when(z - r >= 0)
                def _():
                    arrived(from_left, p, core)

                    @pl.when(z < n_z - 1)
                    def _():
                        copy(from_left, p, RIGHT).start()

                    copy(from_left, p, SIBLING).start()

                @pl.when(z + r < n_z)
                def _():
                    arrived(from_right, p, core)

                    @pl.when(z > 0)
                    def _():
                        copy(from_right, p, LEFT).start()

                    copy(from_right, p, SIBLING).start()

                @pl.when(over_y(r, p))
                def _():
                    copy(nearest[r] * 2 + y, p, ACROSS).start()

            @pl.when(over_y(r - 1, p))
            def _():
                c = nearest[r - 1] * 2 + far
                arrived(c, p, core)
                copy(c, p, SIBLING).start()

            ready = blocks_of(r - 1)
            if p < len(ready):
                guarded(compute, *ready[p])
            if r > 1 and p == pieces - 1:
                for cond, c in blocks_of(r - 2):
                    guarded(finish, cond, c)

        if r == n_z - 1:
            own_far = z * 2 + far
            for p in lent_pieces:
                @pl.when(lend_left)
                def _():
                    copy(own_far, p, LEFT).start()

                @pl.when(lend_right)
                def _():
                    copy(own_far, p, RIGHT).start()

    lent_chip = lent * 2 + far
    for p in lent_pieces:
        arrived(lent_chip, p, core)
        copy(lent_chip, p, SIBLING).start()
    for cond, c in blocks_of(n_z - 1):
        guarded(finish, cond, c)
    last = blocks_of(n_z)
    for cond, c in last:
        guarded(compute, cond, c)
    compute(lent_chip)
    for cond, c in last:
        guarded(finish, cond, c)
    finish(lent_chip)

    for zz in range(n_z):
        for p in range(pieces):
            own, other = zz * 2 + y, zz * 2 + far

            @pl.when((z > 0) & (z <= zz))
            def _():
                copy(own, p, LEFT).wait_send()

            @pl.when((z < n_z - 1) & (z >= zz))
            def _():
                copy(own, p, RIGHT).wait_send()

            if p in lent_pieces:
                @pl.when((zz == z) & lend_left)
                def _():
                    copy(other, p, LEFT).wait_send()

                @pl.when((zz == z) & lend_right)
                def _():
                    copy(other, p, RIGHT).wait_send()

                @pl.when(zz != lent)
                def _():
                    copy(own, p, ACROSS).wait_send()
            else:
                copy(own, p, ACROSS).wait_send()
            copy(own, p, SIBLING).wait_send()
            copy(other, p, SIBLING).wait_send()
    for c in range(n_z * 2):
        for d in range(1, n_width):
            x_copy(d, c).wait_send()


def per_device(tokens, panel_weights, panel_scales, doc_lengths):
    n_seq, n_width = lax.axis_size("seq"), lax.axis_size("width")
    n_tok, depth = tokens.shape
    cols = panel_weights.shape[2]
    share = n_tok // n_width
    chips = n_seq // 2
    pieces = 4
    chunk = min(128, panel_scales.shape[1])
    bf16, f32 = jnp.bfloat16, jnp.float32
    blocks = pl.pallas_call(
        functools.partial(kernel, n_seq, n_width, pieces),
        out_shape=jax.ShapeDtypeStruct((chips, share, 2 * cols), f32),
        in_specs=[
            pl.BlockSpec(memory_space=pl.ANY),
            pl.BlockSpec(memory_space=pltpu.VMEM),
            pl.BlockSpec(memory_space=pl.ANY),
        ],
        out_specs=pl.BlockSpec(memory_space=pltpu.VMEM),
        scratch_shapes=[
            pltpu.VMEM((chips, 2, 2, cols, depth), bf16),
            pltpu.VMEM((n_tok, depth), bf16),
            pltpu.VMEM((chunk, chunk * GROUP), bf16),
            pltpu.VMEM((n_tok, 4 * cols), f32),
            pltpu.VMEM((chips, share, 2 * cols), f32),
            pltpu.VMEM((max(n_width - 1, 1), chips, share, 4 * cols), bf16),
            pltpu.VMEM((max(n_width - 1, 1), chips, share, 4 * cols), bf16),
            pltpu.SemaphoreType.DMA((4, chips, pieces)),
            pltpu.SemaphoreType.DMA((2, chips, pieces)),
            pltpu.SemaphoreType.DMA((max(n_width - 1, 1), chips)),
            pltpu.SemaphoreType.DMA((max(n_width - 1, 1), chips)),
            pltpu.SemaphoreType.DMA((2,)),
            pltpu.SemaphoreType.DMA,
        ],
        compiler_params=pltpu.CompilerParams(
            collective_id=0, has_side_effects=True, vmem_limit_bytes=62 * 1024 * 1024
        ),
        cost_estimate=pl.CostEstimate(
            flops=2 * n_tok * depth * 2 * cols * n_seq,
            bytes_accessed=2 * n_tok * depth + 4 * cols * depth,
            transcendentals=share * cols * n_seq,
        ),
    )(jnp.swapaxes(panel_weights, 1, 2), jnp.swapaxes(panel_scales, 1, 2), tokens)
    mixed = jnp.transpose(blocks, (1, 0, 2)).reshape(share, cols * n_seq)
    position = lax.axis_index("width") * share + jnp.arange(share, dtype=jnp.int32)
    keep = position < jnp.sum(doc_lengths)
    return jnp.where(keep[:, None], mixed, jnp.zeros_like(mixed))


def solution(mesh):
    in_specs = (P("seq", "width"), P(None, "width", "seq"), P(None, "width", "seq"), P("seq", None))
    out_specs = P(("seq", "width"), None)
    return jax.shard_map(
        per_device, mesh=mesh, in_specs=in_specs, out_specs=out_specs, check_vma=False
    )
```

time: 484 us -> 203 us (0.42)
  waiting for transfers between devices: 302 us -> 0 us
  Pallas kernels: 0 us -> 194 us
  local copies, waits for them, and re-layouts: 92.1 us -> 4.8 us
  matrix products: 43.7 us -> 0 us
  other arithmetic: 30.1 us -> 3.56 us
  between operations: 13.1 us -> 0.02 us
    all_gather x2 -> x0, waiting for transfers between devices: 204 us -> none  [gathered_then(): whole = lax.all_gather(x, axis, axis=dim, tiled=True)]
    pallas_call x0 -> x1, Pallas kernels: none -> 194 us  [per_device(): pl.pallas_call(functools.partial(kernel, n_seq, n_width, pieces), out_sha...]
    reduce_scatter x1 -> x0, waiting for transfers between devices: 97.5 us -> none  [per_device(): summed = lax.psum_scatter(summed, 'width', scatter_dimension=0, tiled=True)]
    all_gather x1 -> x0, local copies, waits for them, and re-layouts: 80.4 us -> none  [gathered_then(): whole = lax.all_gather(x, axis, axis=dim, tiled=True)]
    dot_general x1 -> x0, matrix products: 43.7 us -> none  [product(): jnp.einsum('td,gdc->tgc', tokens, weights_deq, preferred_element_type=jnp...]
    convert_element_type x2 -> x0, other arithmetic: 26 us -> none  [the longest x1 24.4 us: product(): weights_deq = (weights.astype(jnp.float32) * spread).astype(jnp.bfloat16)]
    unnamed x3 -> x0, local copies, waits for them, and re-layouts: 5.71 us -> none
  transfers between devices with their start and end apart: 3 -> 0, of which waited for: 3 -> 0; matrix products, arithmetic and copies ran while one was open for 2% -> 0% of each run, Pallas kernels for 0% -> 0%
where the time goes in v1:
time: 203 us
  Pallas kernels  194 us (96%)
  local copies, waits for them, and re-layouts  4.8 us (2%)
  other arithmetic  3.56 us (2%)
    pallas_call x1, Pallas kernels, per_device(): pl.pallas_call(functools.partial(kernel, n_seq, n_width, pieces), out_sha...  194 us

profile of v1, /device:TPU:0, one launch (start us, length us, event | category | flops | bytes accessed | tf_op | source)
XLA Modules:
  0.0 202.7 jit_solution(716750248718268285)
XLA Ops:
  0.0 1.3 reduce_sum.9
  1.3 0.7 add_compare_fusion
  2.0 194.3 %shard_map.46 = f32[8,512,128]{2,1,0:T(8,128)} custom-call(bf16[2,64,8192]{2,1,0:T(8,128)(2,1)} %bitcast.6, f32[2,64,512]{2,1,0:T(8,128)} %bitcast.7, bf16[1024,8192]{1,0:T(8,128)(2,1)} %tokens.1), custom_call_target="tpu_custom_call" | custom-call | flops 34359738368 | bytes 18874368 | tf_op jit(solution)/shard_map/pallas_call | solution.py:316
  196.3 1.9 copy.5
  198.2 1.6 bitcast_select_fusion
  199.8 2.9 %copy.6 = f32[512,1024]{1,0:T(8,128)} copy(f32[512,1024]{0,1:T(8,128)} %bitcast_select_fusion) | data formatting | bytes 4194304 | tf_op jit(solution)/shard_map/jit(_where)/select_n | solution.py:352

commit v2 on v1

--- a/solution.py
+++ b/solution.py
@@ -21,8 +21,8 @@
 
 def kernel(
     n_seq, n_width, pieces,
-    weights, scales, tokens, out,
-    gathered, tok, spread_mat, acc, keep_up, send_buf, recv_buf,
+    weights, scales, tokens, doc_lengths, out,
+    gathered, tok, spread_mat, acc, kept, send_buf, recv_buf,
     send_sem, recv_sem, x_send, x_recv, w_sem, tok_sem,
 ):
     n_z = n_seq // 4
@@ -72,13 +72,15 @@
         )
 
     w_copies = [
-        pltpu.make_async_copy(weights.at[g], gathered.at[chip, g, core], w_sem.at[g])
-        for g in range(2)
+        pltpu.make_async_copy(
+            weights.at[p // per_half, pl.ds((p % per_half) * r_piece, r_piece), :],
+            block(chip, p, core), w_sem.at[p],
+        )
+        for p in range(pieces)
     ]
     for c in w_copies:
         c.start()
     tok_copy = pltpu.make_async_copy(tokens, tok, tok_sem)
-    tok_copy.start()
 
     barrier = pltpu.get_barrier_semaphore()
     for way in range(4):
@@ -101,8 +103,7 @@
 
     for p in range(pieces):
         g, row = p // per_half, (p % per_half) * r_piece
-        if p % per_half == 0:
-            w_copies[g].wait()
+        w_copies[p].wait()
 
         @pl.loop(0, scales.shape[2] // chunk)
         def _(j):
@@ -130,46 +131,87 @@
 
         copy(chip, p, ACROSS).start()
         copy(chip, p, SIBLING).start()
+        if p == 0:
+            tok_copy.start()
 
     tok_copy.wait()
 
     k_step = min(1024, depth)
+
+    half_cols = n_cols // 2
+    live = doc_lengths[0, 0]
+    for k in range(1, doc_lengths.shape[1]):
+        live = live + doc_lengths[0, k]
+    position = wid * share + lax.broadcasted_iota(jnp.int32, (share, half_cols), 0)
+    keep = position < live
+
+    def multiply(load, slot):
+        def rows_of(w):
+            at_rows = pl.ds(pl.multiple_of(w * share, share), share)
+
+            def dot(k):
+                at = pl.ds(pl.multiple_of(k * k_step, k_step), k_step)
+                return lax.dot_general(
+                    tok[at_rows, at], load(at), (((1,), (1,)), ((), ())),
+                    preferred_element_type=jnp.float32,
+                )
+
+            acc[...] = dot(0)
+
+            @pl.loop(1, depth // k_step)
+            def _(k):
+                acc[...] += dot(k)
+
+        for d in range(1, n_width):
+            rows_of(lax.rem(wid + d, n_width))
+            send_buf[d - 1, slot] = acc[...].astype(jnp.bfloat16)
+            x_copy(d, slot).start()
+        rows_of(wid)
+        kept[slot] = acc[...]
+
+    def total(slot):
+        value = kept[slot]
+        for d in range(1, n_width):
+            x_copy(d, slot).wait_recv()
+            value = value + recv_buf[d - 1, slot].astype(jnp.float32)
+        return value
+
+    def store(c, gate, up):
+        mixed = jnp.where(keep, gate / (1.0 + jnp.exp(-gate)) * up, 0.0)
+        if half_cols % 128 == 0:
+            out[:, pl.ds(pl.multiple_of(c * half_cols, half_cols), half_cols)] = mixed
+        else:
+            for at in range(n_z * 2):
+                @pl.when(c == at)
+                def _():
+                    out[:, at * half_cols:(at + 1) * half_cols] = mixed
 
     def compute(c):
         for p in range(pieces):
             arrived(c, p, 1 - core)
-
-        def dot(k):
-            at = pl.ds(pl.multiple_of(k * k_step, k_step), k_step)
-            b = gathered[c, :, :, :, at].reshape(n_cols, k_step)
-            return lax.dot_general(
-                tok[:, at], b, (((1,), (1,)), ((), ())), preferred_element_type=jnp.float32
+        multiply(lambda at: gathered[c, :, :, :, at].reshape(n_cols, k_step), c)
+
+    def finish(c):
+        value = total(c)
+        store(c, value[:, :half_cols], value[:, half_cols:])
+
+    def compute_pair(first, second, g):
+        for p in range(g * per_half, (g + 1) * per_half):
+            arrived(first, p, 1 - core)
+            arrived(second, p, 1 - core)
+
+        def load(at):
+            return jnp.concatenate(
+                [gathered[c, g, :, :, at].reshape(half_cols, k_step) for c in (first, second)],
+                axis=0,
             )
 
-        acc[...] = dot(0)
-
-        @pl.loop(1, depth // k_step)
-        def _(k):
-            acc[...] += dot(k)
-
-        mine = pl.ds(pl.multiple_of(wid * share, share), share)
-        half_cols = n_cols // 2
-        out[c] = acc[mine, :half_cols]
-        keep_up[c] = acc[mine, half_cols:]
-        for d in range(1, n_width):
-            other = pl.ds(pl.multiple_of(lax.rem(wid + d, n_width) * share, share), share)
-            send_buf[d - 1, c] = acc[other, :].astype(jnp.bfloat16)
-            x_copy(d, c).start()
-
-    def finish(c):
-        half_cols = n_cols // 2
-        for d in range(1, n_width):
-            x_copy(d, c).wait_recv()
-        gate, up = out[c], keep_up[c]
-        for d in range(1, n_width):
-            both = recv_buf[d - 1, c].astype(jnp.float32)
-            gate, up = gate + both[:, :half_cols], up + both[:, half_cols:]
-        out[c] = gate / (1.0 + jnp.exp(-gate)) * up
+        multiply(load, (first, second)[g])
+
+    def finish_pair(first, second):
+        gate, up = total(first), total(second)
+        store(first, gate[:, :half_cols], up[:, :half_cols])
+        store(second, gate[:, half_cols:], up[:, half_cols:])
 
     orders = []
     for zz in range(n_z):
@@ -204,6 +246,7 @@
         def _():
             f(c)
 
+    lent_chip, last_chip = lent * 2 + far, nearest[n_z - 1] * 2 + far
     for r in range(1, n_z + 1):
         for p in range(pieces):
             if r < n_z:
@@ -239,10 +282,26 @@
                 arrived(c, p, core)
                 copy(c, p, SIBLING).start()
 
+            if r == n_z and p in lent_pieces:
+                arrived(lent_chip, p, core)
+                copy(lent_chip, p, SIBLING).start()
+
             ready = blocks_of(r - 1)
-            if p < len(ready):
+            if r == n_z:
+                if p == 0:
+                    for cond, c in ready[:2]:
+                        guarded(compute, cond, c)
+                elif p == per_half - 1:
+                    for cond, c in ready[2:]:
+                        guarded(compute, cond, c)
+                elif p == pieces * 5 // 8:
+                    compute_pair(last_chip, lent_chip, 0)
+                    for old in (r - 2, r - 1):
+                        for cond, c in blocks_of(old):
+                            guarded(finish, cond, c)
+            elif p < len(ready):
                 guarded(compute, *ready[p])
-            if r > 1 and p == pieces - 1:
+            if 1 < r < n_z and p == pieces - 1:
                 for cond, c in blocks_of(r - 2):
                     guarded(finish, cond, c)
 
@@ -257,19 +316,8 @@
                 def _():
                     copy(own_far, p, RIGHT).start()
 
-    lent_chip = lent * 2 + far
-    for p in lent_pieces:
-        arrived(lent_chip, p, core)
-        copy(lent_chip, p, SIBLING).start()
-    for cond, c in blocks_of(n_z - 1):
-        guarded(finish, cond, c)
-    last = blocks_of(n_z)
-    for cond, c in last:
-        guarded(compute, cond, c)
-    compute(lent_chip)
-    for cond, c in last:
-        guarded(finish, cond, c)
-    finish(lent_chip)
+    compute_pair(last_chip, lent_chip, 1)
+    finish_pair(last_chip, lent_chip)
 
     for zz in range(n_z):
         for p in range(pieces):
@@ -313,28 +361,29 @@
     pieces = 4
     chunk = min(128, panel_scales.shape[1])
     bf16, f32 = jnp.bfloat16, jnp.float32
-    blocks = pl.pallas_call(
+    return pl.pallas_call(
         functools.partial(kernel, n_seq, n_width, pieces),
-        out_shape=jax.ShapeDtypeStruct((chips, share, 2 * cols), f32),
+        out_shape=jax.ShapeDtypeStruct((share, cols * n_seq), f32),
         in_specs=[
             pl.BlockSpec(memory_space=pl.ANY),
             pl.BlockSpec(memory_space=pltpu.VMEM),
             pl.BlockSpec(memory_space=pl.ANY),
+            pl.BlockSpec(memory_space=pltpu.SMEM),
         ],
         out_specs=pl.BlockSpec(memory_space=pltpu.VMEM),
         scratch_shapes=[
             pltpu.VMEM((chips, 2, 2, cols, depth), bf16),
             pltpu.VMEM((n_tok, depth), bf16),
             pltpu.VMEM((chunk, chunk * GROUP), bf16),
-            pltpu.VMEM((n_tok, 4 * cols), f32),
-            pltpu.VMEM((chips, share, 2 * cols), f32),
+            pltpu.VMEM((share, 4 * cols), f32),
+            pltpu.VMEM((chips, share, 4 * cols), f32),
             pltpu.VMEM((max(n_width - 1, 1), chips, share, 4 * cols), bf16),
             pltpu.VMEM((max(n_width - 1, 1), chips, share, 4 * cols), bf16),
             pltpu.SemaphoreType.DMA((4, chips, pieces)),
             pltpu.SemaphoreType.DMA((2, chips, pieces)),
             pltpu.SemaphoreType.DMA((max(n_width - 1, 1), chips)),
             pltpu.SemaphoreType.DMA((max(n_width - 1, 1), chips)),
-            pltpu.SemaphoreType.DMA((2,)),
+            pltpu.SemaphoreType.DMA((pieces,)),
             pltpu.SemaphoreType.DMA,
         ],
         compiler_params=pltpu.CompilerParams(
@@ -345,11 +394,7 @@
             bytes_accessed=2 * n_tok * depth + 4 * cols * depth,
             transcendentals=share * cols * n_seq,
         ),
-    )(jnp.swapaxes(panel_weights, 1, 2), jnp.swapaxes(panel_scales, 1, 2), tokens)
-    mixed = jnp.transpose(blocks, (1, 0, 2)).reshape(share, cols * n_seq)
-    position = lax.axis_index("width") * share + jnp.arange(share, dtype=jnp.int32)
-    keep = position < jnp.sum(doc_lengths)
-    return jnp.where(keep[:, None], mixed, jnp.zeros_like(mixed))
+    )(jnp.swapaxes(panel_weights, 1, 2), jnp.swapaxes(panel_scales, 1, 2), tokens, doc_lengths)
 
 
 def solution(mesh):

time: 203 us -> 189 us (0.931)
  Pallas kernels: 194 us -> 185 us
  other arithmetic: 3.56 us -> 0 us
    pallas_call x1, Pallas kernels: 194 us -> 185 us  [per_device(): pl.pallas_call(functools.partial(kernel, n_seq, n_width, pieces), out_sha...]
    unnamed x0 -> x1, local copies, waits for them, and re-layouts: none -> 3.16 us
    select_n x1 -> x0, local copies, waits for them, and re-layouts: 2.88 us -> none  [per_device(): return jnp.where(keep[:, None], mixed, jnp.zeros_like(mixed))]
where the time goes in v2:
time: 189 us
  Pallas kernels  185 us (98%)
  local copies, waits for them, and re-layouts  3.16 us (2%)
    pallas_call x1, Pallas kernels, per_device(): pl.pallas_call(functools.partial(kernel, n_seq, n_width, pieces), out_sha...  185 us

profile of v2, /device:TPU:0, one launch (start us, length us, event | category | flops | bytes accessed | tf_op | source)
XLA Modules:
  0.0 188.5 jit_solution(14990139320900374674)
XLA Ops:
  0.0 185.4 %shard_map.46 = f32[512,1024]{1,0:T(8,128)} custom-call(bf16[2,64,8192]{2,1,0:T(8,128)(2,1)} %bitcast.2, f32[2,64,512]{2,1,0:T(8,128)} %bitcast.3, bf16[1024,8192]{1,0:T(8,128)(2,1)} %tokens.1, s32[1,8]{1,0:T(1,128)} %doc_lengths.1), custom_call_target="tpu_custom_call" | custom-call | flops 34359738368 | bytes 18874368 | tf_op jit(solution)/shard_map/pallas_call | solution.py:364
  185.4 3.2 %copy.6 = f32[512,1024]{1,0:T(8,128)} copy(f32[512,1024]{1,0:T(8,128)} %shard_map.46) | data formatting | bytes 4194304
